TPU v7x, 256 devices: a whole 4x4x8 slice. The times are simulated.
256 devices in a mesh: dp: 16 (over x, z_hi, core), fsdp: 16 (over y, z_lo).
Axes of the slice: x: 4, y: 4, z: 8 (z_hi: 2, z_lo: 4; z = z_hi * 4 + z_lo), core: 2. Of those that a mesh axis runs over, the one named last changes fastest.
Arguments:
- query_key_value: bfloat16 [3, 114688, 1664], P(None, ('dp', 'fsdp')), may hold values from -60 to 60
- cotangent: bfloat16 [114688, 3200], P(('dp', 'fsdp')), may hold values from -24 to 24
- proj_weight: bfloat16 [1664, 3200], P('fsdp'), may hold values from -0.15625 to 0.15625
- layer_scale: float32 [3200], replicated, may hold values from 0.3 to 3
- lengths: int32 [16, 16, 4], P(None, 'fsdp'), may hold values from 0 to 192, as said below
Outputs:
- grad_qkv: bfloat16 [3, 114688, 1664], P(None, ('dp', 'fsdp'))
- grad_proj: float32 [1664, 3200], P('fsdp', 'dp')
Inputs may be any that keep to these rules, and one draw needn't show every extreme that they name: lengths[a, b, 0] + lengths[a, b, 1] = 256, each at least 64; lengths[a, b, 2] and lengths[a, b, 3] are both 0 or both from 64 to 96; of the devices a and a + 16 / 2 (a < 8) of one fsdp index exactly one has them nonzero; in every fsdp index the nonzero one of the pair a = 0 has lengths[., b, 3] = 96.
All inputs are finite; a program needn't handle non-finite values.
Results may differ from a plain program's by a relative error of at most 0.011.
Values may be sent and summed in bfloat16 or wider, within the bound.
A program may use at most 128 MiB of HBM per device.

v0:
```python
import jax
import jax.numpy as jnp
from jax import lax
from jax.sharding import PartitionSpec as P

HS = 128
MAIN = 256
SLOT = 96


def slot_ids(count, label):
    slot_pos = jnp.arange(SLOT, dtype=jnp.int32)
    return jnp.where(slot_pos < count, label, -1).astype(jnp.int32)


def attend(query_rows, key_rows, value_rows, grad_rows, segment):
    rows = query_rows.shape[0]
    width = query_rows.shape[1]
    heads = width // HS
    factor = HS ** (-0.5)
    query_h = query_rows.reshape(rows, heads, HS)
    key_h = key_rows.reshape(rows, heads, HS)
    value_h = value_rows.reshape(rows, heads, HS)
    grad_h = grad_rows.reshape(rows, heads, HS)
    scores = jnp.einsum("qhd,khd->hqk", query_h, key_h, preferred_element_type=jnp.float32) * factor
    valid = segment >= 0
    allowed = (segment[:, None] == segment[None, :]) & valid[:, None]
    scores = jnp.where(allowed[None], scores, -1e30)
    highest = jnp.max(scores, axis=2, keepdims=True)
    weights = jnp.exp(scores - highest)
    probs = weights / jnp.sum(weights, axis=2, keepdims=True)
    probs = jnp.where(valid[None, :, None], probs, jnp.zeros_like(probs))
    probs_b = probs.astype(jnp.bfloat16)
    attended = jnp.einsum("hqk,khd->qhd", probs_b, value_h, preferred_element_type=jnp.float32)
    attended = attended.reshape(rows, width).astype(jnp.bfloat16)
    dprob = jnp.einsum("qhd,khd->hqk", grad_h, value_h, preferred_element_type=jnp.float32)
    delta = jnp.sum(probs * dprob, axis=2, keepdims=True)
    dscore = (probs * (dprob - delta) * factor).astype(jnp.bfloat16)
    grad_query = jnp.einsum("hqk,khd->qhd", dscore, key_h, preferred_element_type=jnp.float32)
    grad_key = jnp.einsum("hqk,qhd->khd", dscore, query_h, preferred_element_type=jnp.float32)
    grad_value = jnp.einsum("hqk,qhd->khd", probs_b, grad_h, preferred_element_type=jnp.float32)
    return (
        attended,
        grad_query.reshape(rows, width).astype(jnp.bfloat16),
        grad_key.reshape(rows, width).astype(jnp.bfloat16),
        grad_value.reshape(rows, width).astype(jnp.bfloat16),
    )


def local(query_key_value, cotangent, proj_weight, layer_scale, lengths):
    member = lax.axis_index("dp")
    table = lengths[:, 0, :]
    counts = lax.dynamic_index_in_dim(table, member, 0, keepdims=False)
    scaled = (cotangent.astype(jnp.float32) * layer_scale[None, :]).astype(jnp.bfloat16)
    grad_out = lax.dot_general(
        scaled,
        lax.all_gather(proj_weight, "fsdp", axis=0, tiled=True),
        (((1,), (1,)), ((), ())),
        preferred_element_type=jnp.float32,
    ).astype(jnp.bfloat16)
    stop_first = MAIN + SLOT
    main_pos = jnp.arange(MAIN, dtype=jnp.int32)
    main_seg = (main_pos >= counts[0]).astype(jnp.int32)
    main_res = attend(
        query_key_value[0][:MAIN],
        query_key_value[1][:MAIN],
        query_key_value[2][:MAIN],
        grad_out[:MAIN],
        main_seg,
    )
    first_res = attend(
        query_key_value[0][MAIN:stop_first],
        query_key_value[1][MAIN:stop_first],
        query_key_value[2][MAIN:stop_first],
        grad_out[MAIN:stop_first],
        slot_ids(counts[2], 2),
    )
    second_res = attend(
        query_key_value[0][stop_first:],
        query_key_value[1][stop_first:],
        query_key_value[2][stop_first:],
        grad_out[stop_first:],
        slot_ids(counts[3], 3),
    )
    joined = [
        jnp.concatenate([main_res[index], first_res[index], second_res[index]], axis=0)
        for index in range(4)
    ]
    attended = joined[0]
    partial_rows = lax.psum_scatter(
        lax.dot_general(
            attended, scaled, (((0,), (0,)), ((), ())), preferred_element_type=jnp.float32
        ),
        "fsdp",
        scatter_dimension=0,
        tiled=True,
    )
    grad_proj = lax.psum_scatter(partial_rows, "dp", scatter_dimension=1, tiled=True)
    return (jnp.stack([joined[1], joined[2], joined[3]]), grad_proj)


def solution(mesh):
    placed = (
        P(None, ("dp", "fsdp"), None),
        P(("dp", "fsdp"), None),
        P("fsdp", None),
        P(),
        P(None, "fsdp", None),
    )
    return jax.shard_map(
        local,
        mesh=mesh,
        in_specs=placed,
        out_specs=(P(None, ("dp", "fsdp"), None), P("fsdp", "dp")),
        check_vma=False,
    )
```

profile of v0, /device:TPU:1, one launch (start us, length us, event | category | flops | bytes accessed | tf_op | source)
XLA Modules:
  0.0 885.4 jit_solution(13187281716645030469)
XLA Ops:
  7.2 0.7 all-gather.2.cloned.1.call-update
  8.0 2.3 fusion.113
  10.3 1.0 reshape.286
  11.3 1.0 reshape.285
  12.3 1.0 reshape.282
  13.3 1.0 reshape.281
  14.3 1.9 fusion.112
  16.1 1.4 copy.139
  18.3 1.3 reshape.284
  22.2 1.5 fusion.40
  23.7 1.0 fusion.115
  24.8 1.1 fusion.52
  25.9 1.9 copy.133
  29.1 1.5 fusion.39
  30.6 0.9 copy-done.8
  31.5 1.0 fusion.116
  32.5 2.4 fusion.51
  34.9 2.0 copy.132
  37.6 3.1 fusion.117
  40.7 2.6 convolution_convert_fusion.1
  43.9 10.3 %fusion.10 = f32[1664,3200]{1,0:T(8,128)} fusion(bf16[448,3200]{1,0:T(8,128)(2,1)S(1)} %copy-done.15, f32[3200]{0:T(1024)S(1)} %copy-done.16, bf16[96,1664]{0,1:T(8,128)(2,1)S(1)} %bitcast.107, bf16[96,1664]{0,1:T(8,128)(2,1)S(1)} %bitcast.108, bf16[256,1664]{0,1:T(8,128)(2,1)S(1)} %bitcast.109), kind=kOutput, calls=%fused_computation.16 | convolution fusion | flops 4779794432 | bytes 25670144 | tf_op jit(solution)/shard_map/dot_general | solution.py:91
  56.1 190.5 %all-gather.2.cloned.1.call-done = bf16[1664,3200]{1,0:T(8,128)(2,1)} async-done(((bf16[104,3200]{1,0:T(8,128)(2,1)}), bf16[1664,3200]{1,0:T(8,128)(2,1)}) %all-gather.2.cloned.1.call-update) | async-done | bytes 10649616 | tf_op jit(solution)/shard_map/all_gather | solution.py:57
  246.6 11.2 %convolution_convert_fusion = bf16[448,1664]{1,0:T(8,128)(2,1)S(1)} fusion(bf16[1664,3200]{1,0:T(8,128)(2,1)} %all-gather.2.cloned.1.call-done, bf16[448,3200]{1,0:T(8,128)(2,1)} %param.6, f32[3200]{0:T(1024)S(1)} %copy-done.16), kind=kOutput, calls=%fused_computation.14 | convolution fusion | flops 4776067072 | bytes 15020544 | tf_op jit(solution)/shard_map/dot_general | solution.py:55
  257.8 1.2 copy-done.2
  259.7 3.8 convolution_convert_fusion.2
  263.6 2.3 copy.109
  265.8 2.4 fusion.118
  268.2 7.5 fusion.30
  275.7 1.5 copy.103
  277.3 6.3 fusion.27
  284.3 1.1 slice_bitcast_fusion.1
  285.4 1.2 fusion.66
  286.6 3.1 fusion.48
  289.7 1.2 fusion.69
  290.9 3.1 fusion.47
  294.0 1.7 fusion.54
  295.7 1.6 fusion.53
  297.4 3.0 fusion.50
  300.3 2.9 fusion.49
  303.3 1.3 maximum_bitcast_fusion.2
  304.6 0.8 copy_bitcast_fusion.2
  305.4 389.3 %reduce-scatter.6.cloned.1.call-done = f32[104,3200]{1,0:T(8,128)} async-done(((f32[1664,3200]{1,0:T(8,128)}), f32[104,3200]{1,0:T(8,128)}) %reduce-scatter.6.cloned.1.call-update) | async-done | bytes 1331216
  694.8 1.1 maximum_bitcast_fusion.1
  695.8 1.1 copy_bitcast_fusion.4
  697.1 2.4 pad_maximum_fusion
  699.5 177.6 %all-reduce.4.cloned.1.call-done = f32[104,3200]{1,0:T(8,128)} async-done(((f32[104,3200]{1,0:T(8,128)}), f32[104,3200]{1,0:T(8,128)}) %all-reduce.4.cloned.1.call-update) | async-done | bytes 1331216
  877.1 1.0 constant_dynamic-slice_fusion
  878.1 0.7 copy.119
  (58 shorter events, 8.8 us)
Async XLA Ops:
  7.2 13.0 %copy-start = (s32[16,1,4]{0,2,1:T(4,128)S(1)}, s32[16,1,4]{0,2,1:T(4,128)}, u32[]{:S(2)}) copy-start(s32[16,1,4]{0,2,1:T(4,128)} %param.9) | copy-start | bytes 772
  7.2 239.4 %all-gather.2.cloned.1.call-start = ((), (), s32[]{:S(2)}) async-start(), calls=%async_computation.1 | async-start | bytes 11315200 | tf_op jit(solution)/shard_map/all_gather | solution.py:57
  7.9 686.8 %reduce-scatter.6.cloned.1.call-start = ((), (), s32[]{:S(2)}) async-start(), calls=%async_computation.3 | async-start | bytes 22630400
  18.1 19.6 %copy-start.3 = (bf16[1,256,1664]{1,2,0:T(8,128)(2,1)}, bf16[1,256,1664]{1,2,0:T(8,128)(2,1)S(1)}, u32[]{:S(2)}) copy-start(bf16[1,256,1664]{1,2,0:T(8,128)(2,1)S(1)} %copy.138) | copy-start | bytes 2555908
  23.7 5.3 copy-start.7
  29.1 8.6 copy-start.5
  30.6 0.9 copy-start.8
  40.7 2.6 copy-start.9
  40.7 2.6 copy-start.10
  40.7 3.1 copy-start.15
  40.7 3.1 copy-start.16
  54.1 0.7 copy-start.17
  54.2 822.9 %all-reduce.4.cloned.1.call-start = ((), (), s32[]{:S(2)}) async-start(), calls=%async_computation.2 | async-start | bytes 2662400
  257.8 1.2 copy-start.2
  263.6 4.7 copy-start.6
  268.2 9.0 %copy-start.4 = (bf16[1,256,1664]{1,2,0:T(8,128)(2,1)S(1)}, bf16[1,256,1664]{1,2,0:T(8,128)(2,1)}, u32[]{:S(2)}) copy-start(bf16[1,256,1664]{1,2,0:T(8,128)(2,1)} %copy-done.3) | copy-start | bytes 2555908
  294.0 3.4 copy-start.12
  295.7 4.6 copy-start.11
  303.2 1.4 copy-start.13
  303.2 1.4 copy-start.14
  697.0 181.9 %copy-start.1 = (s32[16,1,4]{0,2,1:T(4,128)S(1)}, s32[16,1,4]{0,2,1:T(4,128)}, u32[]{:S(2)}) copy-start(s32[16,1,4]{0,2,1:T(4,128)} %param.9) | copy-start | bytes 772
Sparse Core Ops, SparseCore 0:
  9.8 236.7 all-gather.1
  249.2 445.5 reduce-scatter.5
  697.4 179.6 all-reduce.3
where the time goes:
time: 889 us; the launch traced here: 885 us
  waiting for transfers between devices  758 us (85%)
  matrix products  71.5 us (8%)
  local copies, waits for them, and re-layouts  30.3 us (3%)
  between operations  14.8 us (2%)
  other arithmetic  10.3 us (1%)
    unnamed x5, waiting for transfers between devices  568 us
    all_gather x1, waiting for transfers between devices, local(): lax.all_gather(proj_weight, 'fsdp', axis=0, tiled=True)  191 us
  transfers between devices with their start and end apart: 3, of which 3 were waited for; matrix products, arithmetic and copies ran while one was open for 12% of the time, Pallas kernels for 0%

commit v1 on v0

v1 whole, which is shorter than its diff:
```python
import jax
import jax.numpy as jnp
from jax import lax
from jax.experimental import pallas as pl
from jax.experimental.pallas import tpu as pltpu
from jax.sharding import PartitionSpec as P

HS = 128
HEADS = 13
HD = HS * HEADS
D = 3200
MAIN = 256
SLOT = 96
TAIL = 2 * SLOT
ROWS = MAIN + TAIL
SHARD = HD // 16
HALF = 13 * 128
FIRST = 7 * 128
LAST = HALF - FIRST
WIN = 7 * 128
STEP = 6 * 128
CHUNK = 208
FACTOR = HS ** (-0.5)
MESH = pl.DeviceIdType.MESH
F32 = jnp.float32
BF16 = jnp.bfloat16

A1, B1, A2, A3, B2, B3 = 0, 3, 7, 9, 11, 13
COT, ATT, GRAD, XS, YS, ZS, FIN = 15, 16, 20, 21, 33, 36, 43
N_MSG = 44


def dot_nn(a, b):
    return lax.dot_general(a, b, (((1,), (0,)), ((), ())), preferred_element_type=F32)


def dot_nt(a, b):
    return lax.dot_general(a, b, (((1,), (1,)), ((), ())), preferred_element_type=F32)


def dot_tn(a, b):
    return lax.dot_general(a, b, (((0,), (0,)), ((), ())), preferred_element_type=F32)


def kernel(
    qkv_hbm, cot_hbm, w_hbm, scale_ref, lens_ref, grad_hbm, proj_ref,
    qkv, scaled, att, p_main, p_tail, w_a, w_b, w_all, go_own, go_out, go_in,
    x_own, x_in, y_own, y_in, z_own, z_in, total, send, recv, local,
):
    dp, member = lax.axis_index("dp"), lax.axis_index("fsdp")
    x, z_hi, core = dp // 4, (dp // 2) % 2, dp % 2
    y, z_lo = member // 4, member % 4
    z = z_hi * 4 + z_lo

    def at_x(k):
        return (lax.rem(x + k, 4) * 4 + z_hi * 2 + core, member)

    def at_y(k):
        return (dp, lax.rem(y + k, 4) * 4 + z_lo)

    def at_z(k):
        t = lax.rem(z + k, 8)
        return (x * 4 + (t // 4) * 2 + core, y * 4 + t % 4)

    sibling = (x * 4 + z_hi * 2 + 1 - core, member)

    def remote(src, dst, index, device):
        return pltpu.make_async_remote_copy(
            src_ref=src, dst_ref=dst, send_sem=send.at[index], recv_sem=recv.at[index],
            device_id=device, device_id_type=MESH,
        )

    def launch(*args):
        copy = remote(*args)
        copy.start()
        return copy

    load_qkv = pltpu.make_async_copy(qkv_hbm, qkv, local.at[0])
    load_qkv.start()
    load_cot = pltpu.make_async_copy(cot_hbm, scaled.at[0], local.at[1])
    load_cot.start()

    col = pl.multiple_of(core * (12 * 128), 128)
    part_a = w_hbm.at[:, pl.ds(col, FIRST)]
    part_b = w_hbm.at[:, pl.ds(col + FIRST, LAST)]
    load_a = pltpu.make_async_copy(part_a, w_a.at[z_lo, y], local.at[2])
    load_a.start()
    load_b = pltpu.make_async_copy(part_b, w_b.at[y, z_lo], local.at[3])
    load_b.start()

    peers = [sibling, at_x(1), at_x(3)] + [at_y(k) for k in (1, 2, 3)] + [at_z(k) for k in range(1, 8)]
    barrier = pltpu.get_barrier_semaphore()
    for peer in peers:
        pl.semaphore_signal(barrier, inc=1, device_id=peer, device_id_type=MESH)
    pl.semaphore_wait(barrier, len(peers))

    sent = []
    gather_a = [launch(part_a, w_a.at[z_lo, y], A1 + i, at_y(k)) for i, k in enumerate((1, 3, 2))]
    small = LAST // 2
    gather_b = [launch(part_b, w_b.at[y, z_lo], B1 + i, at_z(k)) for i, k in enumerate((1, 7))]
    for i, k in enumerate((2, 6)):
        piece = w_hbm.at[:, pl.ds(col + FIRST + i * small, small)]
        gather_b.append(launch(piece, w_b.at[y, z_lo, :, pl.ds(i * small, small)], B1 + 2 + i, at_z(k)))
    cot_copy = launch(cot_hbm, scaled.at[1], COT, sibling)
    sent += gather_a + gather_b + [cot_copy]

    first_count = lens_ref[dp, 0]
    count_2, count_3 = lens_ref[dp, 2], lens_ref[dp, 3]

    def main_mask():
        rows = lax.broadcasted_iota(jnp.int32, (MAIN, MAIN), 0)
        cols = lax.broadcasted_iota(jnp.int32, (MAIN, MAIN), 1)
        one = jnp.where(rows >= first_count, 1, 0)
        two = jnp.where(cols >= first_count, 1, 0)
        return one == two

    def tail_mask():
        def ids(axis):
            at = lax.broadcasted_iota(jnp.int32, (TAIL, TAIL), axis)
            first = jnp.where(at < count_2, 2, -1)
            second = jnp.where(at - SLOT < count_3, 3, -1)
            return jnp.where(at < SLOT, first, second)

        one, two = ids(0), ids(1)
        return (one == two) & (one >= 0)

    def soft(query, key, allowed):
        scores = jnp.where(allowed, dot_nt(query, key) * FACTOR, -1e30)
        highest = jnp.max(scores, axis=1, keepdims=True)
        weights = jnp.where(allowed, jnp.exp(scores - highest), 0.0)
        norm = jnp.sum(weights, axis=1, keepdims=True)
        return weights * (1.0 / jnp.where(norm > 0.0, norm, 1.0))

    load_qkv.wait()

    def forward(head, _):
        lanes = pl.ds(pl.multiple_of(head * HS, HS), HS)
        query, key, value = qkv[0, :, lanes], qkv[1, :, lanes], qkv[2, :, lanes]
        probs = soft(query[:MAIN], key[:MAIN], main_mask())
        probs_t = soft(query[MAIN:], key[MAIN:], tail_mask())
        p_main[head] = probs
        p_tail[head] = probs_t
        out = dot_nn(probs.astype(BF16), value[:MAIN])
        out_t = dot_nn(probs_t.astype(BF16), value[MAIN:])
        att[0, lanes, :] = jnp.concatenate([out, out_t], axis=0).T.astype(BF16)
        return 0

    lax.fori_loop(0, HEADS, forward, 0)

    att_copies = []
    for k in range(4):
        rows = pl.ds(pl.multiple_of(416 * k + CHUNK * (1 - core), 16), CHUNK)
        att_copies.append(launch(att.at[0, rows], att.at[1, rows], ATT + k, sibling))
    sent += att_copies

    def scale_rows(part):
        def one(step, _):
            rows = pl.ds(pl.multiple_of(step * 64, 64), 64)
            scaled[part, rows, :] = (scaled[part, rows, :].astype(F32) * scale_ref[...]).astype(BF16)
            return 0

        lax.fori_loop(0, ROWS // 64, one, 0)

    load_cot.wait()
    scale_rows(0)

    load_a.wait()
    load_b.wait()
    for copy in gather_a:
        copy.wait_recv()
    wide_a = [launch(w_a.at[z_lo], w_a.at[z_lo], A2 + i, at_z(k)) for i, k in enumerate((1, 7))]
    for copy in gather_b:
        copy.wait_recv()
    wide_b = [launch(w_b.at[y], w_b.at[y], B2 + i, at_y(k)) for i, k in enumerate((1, 3))]
    sent += wide_a + wide_b

    cot_copy.wait_recv()
    scale_rows(1)
    for copy in att_copies:
        copy.wait_recv()

    hops = []
    for i in range(4):
        block = lax.rem(y + 1 + i, 4)
        way = 1 if i % 2 == 0 else 3
        rows = pl.ds(pl.multiple_of(416 * block + CHUNK * core, 16), CHUNK)
        hop = []
        for j, k in enumerate((2, 4 - way, way, 0)):
            cols = pl.ds(pl.multiple_of(lax.rem(x + k, 4) * STEP, 128), WIN)
            term = dot_nn(att[0, rows, :], scaled[0, :, cols]) + dot_nn(att[1, rows, :], scaled[1, :, cols])
            x_own[i, j] = term.astype(BF16)
            if j < 2:
                hop.append(launch(x_own.at[i, j], x_in.at[i, j], XS + 3 * i + j, at_x(way if j == 0 else 4 - way)))
        hops.append(hop)

    def pass_on(i):
        way = 1 if i % 2 == 0 else 3
        hops[i][0].wait_recv()

        def add(step, _):
            rows = pl.ds(pl.multiple_of(step * 16, 16), 16)
            x_own[i, 2, rows, :] = (x_own[i, 2, rows, :].astype(F32) + x_in[i, 0, rows, :].astype(F32)).astype(BF16)
            return 0

        lax.fori_loop(0, CHUNK // 16, add, 0)
        hops[i].append(launch(x_own.at[i, 2], x_in.at[i, 2], XS + 3 * i + 2, at_x(way)))

    y_copies = []

    def finish_x(i):
        hops[i][1].wait_recv()
        hops[i][2].wait_recv()

        def add(step, _):
            rows = pl.ds(pl.multiple_of(step * 16, 16), 16)
            term = x_own[i, 3, rows, :].astype(F32) + x_in[i, 1, rows, :].astype(F32) + x_in[i, 2, rows, :].astype(F32)
            y_own[i, rows, :] = term.astype(BF16)
            return 0

        lax.fori_loop(0, CHUNK // 16, add, 0)
        if i < 3:
            y_copies.append(launch(y_own.at[i], y_in.at[i], YS + i, at_y(1 + i)))

    pass_on(0)

    wide_a[0].wait_recv()
    behind, ahead = lax.rem(z_lo + 3, 4), lax.rem(z_lo + 1, 4)
    far_a = [launch(w_a.at[behind, pl.ds(0, 2)], w_a.at[behind, pl.ds(0, 2)], A3, at_z(1))]
    wide_a[1].wait_recv()
    far_a.append(launch(w_a.at[ahead, pl.ds(2, 2)], w_a.at[ahead, pl.ds(2, 2)], A3 + 1, at_z(7)))
    behind, ahead = lax.rem(y + 3, 4), lax.rem(y + 1, 4)
    wide_b[0].wait_recv()
    far_b = [launch(w_b.at[behind, pl.ds(0, 2)], w_b.at[behind, pl.ds(0, 2)], B3, at_y(1))]
    wide_b[1].wait_recv()
    far_b.append(launch(w_b.at[ahead, pl.ds(2, 2)], w_b.at[ahead, pl.ds(2, 2)], B3 + 1, at_y(3)))
    sent += far_a + far_b

    pass_on(1)
    finish_x(0)
    for copy in far_a + far_b:
        copy.wait_recv()

    for block in range(4):
        rows = slice(416 * block, 416 * block + 416)
        left = jnp.concatenate([w_a[k, block].astype(F32) for k in range(4)], axis=0)
        w_all[rows, :FIRST] = left.astype(BF16)
        right = jnp.concatenate([w_b[block, k].astype(F32) for k in range(4)], axis=0)
        w_all[rows, FIRST:] = right.astype(BF16)

    keep = jnp.where(core == 1, 0.0, 1.0)
    w_all[:, :128] = (w_all[:, :128].astype(F32) * keep).astype(BF16)

    cols = pl.ds(col, HALF)
    cuts = ((0, 512), (512, 512), (1024, 640))
    for low, size in cuts:
        go_out[:, low:low + size] = dot_nt(scaled[1, :, cols], w_all[low:low + size, :]).astype(BF16)
    go_copy = launch(go_out, go_in, GRAD, sibling)
    sent.append(go_copy)
    for low, size in cuts:
        go_own[:, low:low + size] = dot_nt(scaled[0, :, cols], w_all[low:low + size, :])

    pass_on(2)
    finish_x(1)
    go_copy.wait_recv()

    def grads(query, key, value, grad, probs):
        dprob = dot_nt(grad, value)
        delta = jnp.sum(probs * dprob, axis=1, keepdims=True)
        dscore = (probs * (dprob - delta) * FACTOR).astype(BF16)
        return dot_nn(dscore, key), dot_tn(dscore, query), dot_tn(probs.astype(BF16), grad)

    def backward(head, _):
        lanes = pl.ds(pl.multiple_of(head * HS, HS), HS)
        query, key, value = qkv[0, :, lanes], qkv[1, :, lanes], qkv[2, :, lanes]
        grad = (go_own[:, lanes] + go_in[:, lanes].astype(F32)).astype(BF16)
        main = grads(query[:MAIN], key[:MAIN], value[:MAIN], grad[:MAIN], p_main[head])
        tail = grads(query[MAIN:], key[MAIN:], value[MAIN:], grad[MAIN:], p_tail[head])
        for i in range(3):
            qkv[i, :MAIN, lanes] = main[i].astype(BF16)
            qkv[i, MAIN:, lanes] = tail[i].astype(BF16)
        return 0

    lax.fori_loop(0, HEADS, backward, 0)
    store = pltpu.make_async_copy(qkv, grad_hbm, local.at[0])
    store.start()

    pass_on(3)
    finish_x(2)
    finish_x(3)

    for copy in y_copies:
        copy.wait_recv()
    for part in range(2):
        rows = slice(part * SHARD, part * SHARD + SHARD)
        term = y_own[3, rows, :].astype(F32)
        for k in range(3):
            term = term + y_in[k, rows, :].astype(F32)
        z_own[part] = term.astype(BF16)

    mine = (z_lo // 2) == core
    z_copies = []
    for k in range(1, 8):
        t = lax.rem(z + k, 8)
        to_lo, to_hi = t % 4, t // 4
        wide = pl.ds(pl.multiple_of(to_hi * 384, 128), 512)
        copy = remote(z_own.at[to_lo % 2, :, wide], z_in.at[k - 1], ZS + k - 1, at_z(k))
        goes = (to_lo // 2) == core
        pl.when(goes)(copy.start)
        z_copies.append((goes, copy))
    fin_copy = remote(total, total, FIN, sibling)

    @pl.when(mine)
    def _():
        for _, copy in z_copies:
            copy.wait_recv()
        wide = pl.ds(pl.multiple_of(z_hi * 384, 128), 512)
        term = z_own[z_lo % 2, :, wide].astype(F32)
        for k in range(7):
            term = term + z_in[k].astype(F32)
        total[...] = term
        fin_copy.start()
        fin_copy.wait_send()

    @pl.when(jnp.logical_not(mine))
    def _():
        fin_copy.wait_recv()

    proj_ref[...] = total[...]
    store.wait()
    for goes, copy in z_copies:
        pl.when(goes)(copy.wait_send)
    for copy in sent + y_copies + [c for hop in hops for c in hop]:
        copy.wait_send()


def local_part(query_key_value, cotangent, proj_weight, layer_scale, lengths):
    any_space = pl.BlockSpec(memory_space=pl.ANY)
    vmem = pl.BlockSpec(memory_space=pltpu.VMEM)
    grad, window = pl.pallas_call(
        kernel,
        out_shape=(
            jax.ShapeDtypeStruct((3, ROWS, HD), BF16),
            jax.ShapeDtypeStruct((SHARD, 512), F32),
        ),
        in_specs=[any_space, any_space, any_space, vmem, pl.BlockSpec(memory_space=pltpu.SMEM)],
        out_specs=(any_space, vmem),
        scratch_shapes=[
            pltpu.VMEM((3, ROWS, HD), BF16),
            pltpu.VMEM((2, ROWS, D), BF16),
            pltpu.VMEM((2, HD, ROWS), BF16),
            pltpu.VMEM((HEADS, MAIN, MAIN), F32),
            pltpu.VMEM((HEADS, TAIL, TAIL), F32),
            pltpu.VMEM((4, 4, SHARD, FIRST), BF16),
            pltpu.VMEM((4, 4, SHARD, LAST), BF16),
            pltpu.VMEM((HD, HALF), BF16),
            pltpu.VMEM((ROWS, HD), F32),
            pltpu.VMEM((ROWS, HD), BF16),
            pltpu.VMEM((ROWS, HD), BF16),
            pltpu.VMEM((4, 4, CHUNK, WIN), BF16),
            pltpu.VMEM((4, 3, CHUNK, WIN), BF16),
            pltpu.VMEM((4, CHUNK, WIN), BF16),
            pltpu.VMEM((3, CHUNK, WIN), BF16),
            pltpu.VMEM((2, SHARD, WIN), BF16),
            pltpu.VMEM((7, SHARD, 512), BF16),
            pltpu.VMEM((SHARD, 512), F32),
            pltpu.SemaphoreType.DMA((N_MSG,)),
            pltpu.SemaphoreType.DMA((N_MSG,)),
            pltpu.SemaphoreType.DMA((4,)),
        ],
        compiler_params=pltpu.CompilerParams(
            collective_id=0, has_side_effects=True, vmem_limit_bytes=62 * 2**20
        ),
        name="attention_block",
    )(query_key_value, cotangent, proj_weight, layer_scale.reshape(1, D), lengths.reshape(16, 4))
    dp = lax.axis_index("dp")
    start = (dp // 4) * 32 + ((dp // 2) % 2) * 16 + (dp % 2) * 200
    return grad, lax.dynamic_slice(window, (0, start), (SHARD, 200))


def solution(mesh):
    placed = (
        P(None, ("dp", "fsdp"), None),
        P(("dp", "fsdp"), None),
        P("fsdp", None),
        P(),
        P(None, "fsdp", None),
    )
    return jax.shard_map(
        local_part,
        mesh=mesh,
        in_specs=placed,
        out_specs=(P(None, ("dp", "fsdp"), None), P("fsdp", "dp")),
        check_vma=False,
    )
```

time: 889 us -> 118 us (0.13)
  waiting for transfers between devices: 758 us -> 0 us
  Pallas kernels: 0 us -> 107 us
  matrix products: 71.5 us -> 0 us
  local copies, waits for them, and re-layouts: 30.3 us -> 9.13 us
  between operations: 14.8 us -> 0.7 us
  other arithmetic: 10.3 us -> 0 us
    unnamed x5 -> x0, waiting for transfers between devices: 568 us -> none
    all_gather x1 -> x0, waiting for transfers between devices: 191 us -> none  [local(): lax.all_gather(proj_weight, 'fsdp', axis=0, tiled=True)]
    pallas_call x0 -> x1, Pallas kernels: none -> 107 us  [local_part(): pl.pallas_call(kernel, out_shape=(jax.ShapeDtypeStruct((3, ROWS, HD), BF1...]
    dot_general x19 -> x0, matrix products: 68.4 us -> none  [the longest x3 13.4 us: attend(): jnp.einsum('hqk,qhd->khd', dscore, query_h, preferred_element_type=jnp.fl...]
    convert_element_type x8 -> x0, local copies, waits for them, and re-layouts: 10.3 us -> none  [the longest x2 3.91 us: attend(): attended = attended.reshape(rows, width).astype(jnp.bfloat16)]
  transfers between devices with their start and end apart: 3 -> 0, of which waited for: 3 -> 0; matrix products, arithmetic and copies ran while one was open for 12% -> 0% of each run, Pallas kernels for 0% -> 0%
where the time goes in v1:
time: 118 us; the launch traced here: 117 us
  Pallas kernels  107 us (91%)
  local copies, waits for them, and re-layouts  9.13 us (8%)
    pallas_call x1, Pallas kernels, local_part(): pl.pallas_call(kernel, out_shape=(jax.ShapeDtypeStruct((3, ROWS, HD), BF1...  107 us
    unnamed x2, local copies, waits for them, and re-layouts  5.44 us

profile of v1, /device:TPU:1, one launch (start us, length us, event | category | flops | bytes accessed | tf_op | source)
XLA Modules:
  0.0 117.3 jit_solution(11003443627502599607)
XLA Ops:
  0.7 1.3 %reshape.10.scale_ref = f32[1,3200]{1,0:T(1,128)} reshape(f32[3200]{0:T(1024)} %param.8) | data formatting | bytes 25600 | tf_op jit(solution)/shard_map/reshape | solution.py:374
  2.0 1.4 %copy.7.lens_ref = s32[16,4]{1,0:T(8,128)} copy(s32[16,4]{0,1:T(4,128)} %bitcast.1) | data formatting | bytes 512 | tf_op jit(solution)/shard_map/reshape | solution.py:374
  3.4 107.4 %attention_block.1 = (bf16[3,448,1664]{2,1,0:T(8,128)(2,1)}, f32[104,512]{1,0:T(8,128)}) custom-call(bf16[3,448,1664]{2,1,0:T(8,128)(2,1)} %qkv_hbm.1, bf16[448,3200]{1,0:T(8,128)(2,1)} %cot_hbm.1, bf16[104,3200]{1,0:T(8,128)(2,1)} %w_hbm.1, f32[1,3200]{1,0:T(1,128)} %reshape.10.scale_ref, s32[16,4]{1,0:T(8,128)} %copy.7.lens_ref), custom_call_target="tpu_custom_call" | custom-call | tf_op jit(solution)/shard_map/attention_block/pallas_call | solution.py:339
  110.8 1.0 constant_dynamic-slice_fusion
  111.8 0.7 copy.8
  112.6 4.7 %copy.10 = bf16[3,448,1664]{2,1,0:T(8,128)(2,1)} copy(bf16[3,448,1664]{2,1,0:T(8,128)(2,1)} %get-tuple-element.10) | data formatting | bytes 8945664

commit v2 on v1

v2 whole, which is shorter than its diff:
```python
import jax
import jax.numpy as jnp
from jax import lax
from jax.experimental import pallas as pl
from jax.experimental.pallas import tpu as pltpu
from jax.sharding import PartitionSpec as P

HS = 128
HEADS = 13
HD = HS * HEADS
D = 3200
MAIN = 256
SLOT = 96
TAIL = 2 * SLOT
ROWS = MAIN + TAIL
SHARD = HD // 16
HALF = 13 * 128
FIRST = 7 * 128
LAST = HALF - FIRST
WIN = 7 * 128
STEP = 6 * 128
CHUNK = 208
FACTOR = HS ** (-0.5)
LOG2E = 1.4426950408889634
MESH = pl.DeviceIdType.MESH
F32 = jnp.float32
BF16 = jnp.bfloat16

A1, B1, A2, A3, B2, B3 = 0, 3, 7, 9, 11, 13
COT, ATT, GRAD, XS, YS, ZS, FIN = 15, 20, 24, 25, 49, 55, 76
N_MSG = 77
PARTS = ((0, 512), (512, 384))


def dot_nn(a, b):
    return lax.dot_general(a, b, (((1,), (0,)), ((), ())), preferred_element_type=F32)


def dot_nt(a, b):
    return lax.dot_general(a, b, (((1,), (1,)), ((), ())), preferred_element_type=F32)


def dot_tn(a, b):
    return lax.dot_general(a, b, (((0,), (0,)), ((), ())), preferred_element_type=F32)


def kernel(
    qkv_hbm, cot_hbm, w_hbm, scale_hbm, lens_ref, grad_hbm, proj_ref,
    qkv, scaled, scale, att, bias_main, bias_tail, p_main, p_tail, w_a, w_b, w_all, go_own, go_out, go_in,
    xa_own, xb_own, xa_in, xb_in, ya_own, yb_own, ya_in, yb_in, za, zb, z_in, total, send, recv, local,
):
    dp, member = lax.axis_index("dp"), lax.axis_index("fsdp")
    x, z_hi, core = dp // 4, (dp // 2) % 2, dp % 2
    y, z_lo = member // 4, member % 4
    z = z_hi * 4 + z_lo

    def at_x(k):
        return (lax.rem(x + k, 4) * 4 + z_hi * 2 + core, member)

    def at_y(k):
        return (dp, lax.rem(y + k, 4) * 4 + z_lo)

    def at_z(k):
        t = lax.rem(z + k, 8)
        return (x * 4 + (t // 4) * 2 + core, y * 4 + t % 4)

    sibling = (x * 4 + z_hi * 2 + 1 - core, member)

    def remote(src, dst, index, device):
        return pltpu.make_async_remote_copy(
            src_ref=src, dst_ref=dst, send_sem=send.at[index], recv_sem=recv.at[index],
            device_id=device, device_id_type=MESH,
        )

    def launch(*args):
        copy = remote(*args)
        copy.start()
        return copy

    load_qkv = pltpu.make_async_copy(qkv_hbm, qkv, local.at[0])
    load_qkv.start()
    load_scale = pltpu.make_async_copy(scale_hbm, scale.at[0], local.at[4])
    load_scale.start()
    load_cot = pltpu.make_async_copy(cot_hbm, scaled.at[0], local.at[1])
    load_cot.start()

    col = pl.multiple_of(core * (12 * 128), 128)
    part_a = w_hbm.at[:, pl.ds(col, FIRST)]
    part_b = w_hbm.at[:, pl.ds(col + FIRST, LAST)]
    load_a = pltpu.make_async_copy(part_a, w_a.at[z_lo, y], local.at[2])
    load_a.start()
    load_b = pltpu.make_async_copy(part_b, w_b.at[y, z_lo], local.at[3])
    load_b.start()

    peers = [sibling, at_x(1), at_x(3)] + [at_y(k) for k in (1, 2, 3)] + [at_z(k) for k in range(1, 8)]
    barrier = pltpu.get_barrier_semaphore()
    for peer in peers:
        pl.semaphore_signal(barrier, inc=1, device_id=peer, device_id_type=MESH)
    pl.semaphore_wait(barrier, len(peers))

    windows = [pl.multiple_of(lax.rem(x + k, 4) * STEP, 128) for k in (2, 3, 1, 0)]
    pieces = [pl.ds(low, STEP) for low in windows] + [pl.ds(D - 128, 128)]
    cot_copies = [
        launch(cot_hbm.at[:, piece], scaled.at[1, :, piece], COT + i, sibling) for i, piece in enumerate(pieces)
    ]
    sent = list(cot_copies)

    gather_a = [launch(part_a, w_a.at[z_lo, y], A1 + i, at_y(k)) for i, k in enumerate((1, 3, 2))]
    small = LAST // 2
    gather_b = [launch(part_b, w_b.at[y, z_lo], B1 + i, at_z(k)) for i, k in enumerate((1, 7))]
    for i, k in enumerate((2, 6)):
        piece = w_hbm.at[:, pl.ds(col + FIRST + i * small, small)]
        gather_b.append(launch(piece, w_b.at[y, z_lo, :, pl.ds(i * small, small)], B1 + 2 + i, at_z(k)))
    sent += gather_a + gather_b

    first_count = lens_ref[dp, 0, 0]
    count_2, count_3 = lens_ref[dp, 0, 2], lens_ref[dp, 0, 3]

    def main_mask():
        rows = lax.broadcasted_iota(jnp.int32, (MAIN, MAIN), 0)
        cols = lax.broadcasted_iota(jnp.int32, (MAIN, MAIN), 1)
        one = jnp.where(rows >= first_count, 1, 0)
        two = jnp.where(cols >= first_count, 1, 0)
        return one == two

    def tail_mask():
        def ids(axis):
            at = lax.broadcasted_iota(jnp.int32, (TAIL, TAIL), axis)
            first = jnp.where(at < count_2, 2, -1)
            second = jnp.where(at - SLOT < count_3, 3, -1)
            return jnp.where(at < SLOT, first, second)

        one, two = ids(0), ids(1)
        return (one == two) & (one >= 0)

    bias_main[...] = jnp.where(main_mask(), 0.0, -1e30)
    bias_tail[...] = jnp.where(tail_mask(), 0.0, -1e30)

    def soft(query, key, bias):
        scores = dot_nt(query, key) * (FACTOR * LOG2E) + bias
        highest = jnp.maximum(jnp.max(scores, axis=1, keepdims=True), -1e29)
        weights = jnp.exp2(scores - highest)
        norm = jnp.sum(weights, axis=1, keepdims=True)
        return weights * (1.0 / jnp.where(norm > 0.0, norm, 1.0))

    load_qkv.wait()

    def forward(head, _):
        lanes = pl.ds(pl.multiple_of(head * HS, HS), HS)
        query, key, value = qkv[0, :, lanes], qkv[1, :, lanes], qkv[2, :, lanes]
        probs = soft(query[:MAIN], key[:MAIN], bias_main[...])
        probs_t = soft(query[MAIN:], key[MAIN:], bias_tail[...])
        p_main[head] = probs
        p_tail[head] = probs_t
        out = dot_nn(probs.astype(BF16), value[:MAIN])
        out_t = dot_nn(probs_t.astype(BF16), value[MAIN:])
        att[0, lanes, :] = jnp.concatenate([out, out_t], axis=0).T.astype(BF16)
        return 0

    att_copies = []

    def heads(i):
        block = lax.rem(y + 1 + i, 4)
        low, high = 3 * block, 3 * block + 4
        if i > 0:
            low = low + jnp.where(block > 0, 1, 0)
        if i == 3:
            high = high - jnp.where(block < 3, 1, 0)
        lax.fori_loop(low, high, forward, 0)
        rows = pl.ds(pl.multiple_of(416 * block + CHUNK * (1 - core), 16), CHUNK)
        att_copies.append(launch(att.at[0, rows], att.at[1, rows], ATT + i, sibling))

    def scale_piece(part, piece):
        def one(step, _):
            rows = pl.ds(pl.multiple_of(step * 64, 64), 64)
            scaled[part, rows, piece] = (scaled[part, rows, piece].astype(F32) * scale[:, piece]).astype(BF16)
            return 0

        lax.fori_loop(0, ROWS // 64, one, 0)

    x_own, x_in = (xa_own, xb_own), (xa_in, xb_in)
    y_own, y_in = (ya_own, yb_own), (ya_in, yb_in)
    hops, y_copies, z_copies = [], ([], []), []

    def way_of(i):
        return 1 if i % 2 == 0 else 3

    def multiply(i):
        part, at = i // 4, i % 4
        way = way_of(i)
        rows = pl.ds(pl.multiple_of(416 * lax.rem(y + 1 + at, 4) + CHUNK * core, 16), CHUNK)
        if part == 0:
            att_copies[at].wait_recv()
        hop = []
        low, size = PARTS[part]
        order = (2, 4 - way, way, 0)
        for j, k in enumerate(order):
            if i == 0:
                scale_piece(0, pieces[j])
                cot_copies[j].wait_recv()
                scale_piece(1, pieces[j])
            cols = pl.ds(pl.multiple_of(lax.rem(x + k, 4) * STEP + low, 128), size)
            term = dot_nn(att[0, rows, :], scaled[0, :, cols]) + dot_nn(att[1, rows, :], scaled[1, :, cols])
            x_own[part][at, j] = term.astype(BF16)
            if j < 2:
                to = at_x(way if j == 0 else 4 - way)
                hop.append(launch(x_own[part].at[at, j], x_in[part].at[at, j], XS + 3 * i + j, to))
        hops.append(hop)

    def pass_on(i):
        part, at = i // 4, i % 4
        own, came = x_own[part], x_in[part]
        hops[i][0].wait_recv()

        def add(step, _):
            rows = pl.ds(pl.multiple_of(step * 16, 16), 16)
            own[at, 2, rows, :] = (own[at, 2, rows, :].astype(F32) + came[at, 0, rows, :].astype(F32)).astype(BF16)
            return 0

        lax.fori_loop(0, CHUNK // 16, add, 0)
        hops[i].append(launch(own.at[at, 2], came.at[at, 2], XS + 3 * i + 2, at_x(way_of(i))))

    def finish_x(i):
        part, at = i // 4, i % 4
        own, came, out = x_own[part], x_in[part], y_own[part]
        hops[i][1].wait_recv()
        hops[i][2].wait_recv()

        def add(step, _):
            rows = pl.ds(pl.multiple_of(step * 16, 16), 16)
            term = own[at, 3, rows, :].astype(F32) + came[at, 1, rows, :].astype(F32) + came[at, 2, rows, :].astype(F32)
            out[at, rows, :] = term.astype(BF16)
            return 0

        lax.fori_loop(0, CHUNK // 16, add, 0)
        if at < 3:
            y_copies[part].append(launch(out.at[at], y_in[part].at[at], YS + 3 * part + at, at_y(1 + at)))

    def finish_y(part):
        out = (za, zb)[part]
        for copy in y_copies[part]:
            copy.wait_recv()
        for half in range(2):
            rows = slice(half * SHARD, half * SHARD + SHARD)
            term = y_own[part][3, rows, :].astype(F32)
            for k in range(3):
                term = term + y_in[part][k, rows, :].astype(F32)
            out[half] = term.astype(BF16)
        for k in range(1, 8):
            t = lax.rem(z + k, 8)
            to_lo, to_hi = t % 4, t // 4
            goes = (to_lo // 2) == core
            low, high = goes & (to_hi == 0), goes & (to_hi == 1)
            if part == 0:
                todo = [
                    (low, mine & (z_hi == 0), za.at[to_lo % 2], z_in.at[k - 1], ZS + k - 1),
                    (high, mine & (z_hi == 1), za.at[to_lo % 2, :, pl.ds(384, 128)], z_in.at[k - 1, :, pl.ds(0, 128)], ZS + 6 + k),
                ]
            else:
                todo = [(high, mine & (z_hi == 1), zb.at[to_lo % 2], z_in.at[k - 1, :, pl.ds(128, 384)], ZS + 13 + k)]
            for goes_now, comes, src, dst, index in todo:
                copy = remote(src, dst, index, at_z(k))
                pl.when(goes_now)(copy.start)
                z_copies.append((goes_now, comes, copy))

    mine = (z_lo // 2) == core

    heads(0)
    load_scale.wait()
    load_cot.wait()
    multiply(0)
    heads(1)

    load_a.wait()
    load_b.wait()
    for copy in gather_a:
        copy.wait_recv()
    wide_a = [launch(w_a.at[z_lo], w_a.at[z_lo], A2 + i, at_z(k)) for i, k in enumerate((1, 7))]
    for copy in gather_b:
        copy.wait_recv()
    wide_b = [launch(w_b.at[y], w_b.at[y], B2 + i, at_y(k)) for i, k in enumerate((1, 3))]
    sent += wide_a + wide_b

    multiply(1)
    pass_on(0)
    heads(2)
    multiply(2)
    pass_on(1)
    heads(3)
    multiply(3)
    pass_on(2)

    wide_a[0].wait_recv()
    behind, ahead = lax.rem(z_lo + 3, 4), lax.rem(z_lo + 1, 4)
    far_a = [launch(w_a.at[behind, pl.ds(0, 2)], w_a.at[behind, pl.ds(0, 2)], A3, at_z(1))]
    wide_a[1].wait_recv()
    far_a.append(launch(w_a.at[ahead, pl.ds(2, 2)], w_a.at[ahead, pl.ds(2, 2)], A3 + 1, at_z(7)))
    behind, ahead = lax.rem(y + 3, 4), lax.rem(y + 1, 4)
    wide_b[0].wait_recv()
    far_b = [launch(w_b.at[behind, pl.ds(0, 2)], w_b.at[behind, pl.ds(0, 2)], B3, at_y(1))]
    wide_b[1].wait_recv()
    far_b.append(launch(w_b.at[ahead, pl.ds(2, 2)], w_b.at[ahead, pl.ds(2, 2)], B3 + 1, at_y(3)))
    sent += far_a + far_b

    cot_copies[4].wait_recv()
    scale_piece(0, pieces[4])
    scale_piece(1, pieces[4])
    multiply(4)
    pass_on(3)
    multiply(5)
    finish_x(0)
    finish_x(1)
    for copy in far_a + far_b:
        copy.wait_recv()

    for block in range(4):
        rows = slice(416 * block, 416 * block + 416)
        left = jnp.concatenate([w_a[k, block].astype(F32) for k in range(4)], axis=0)
        w_all[rows, :FIRST] = left.astype(BF16)
        right = jnp.concatenate([w_b[block, k].astype(F32) for k in range(4)], axis=0)
        w_all[rows, FIRST:] = right.astype(BF16)

    keep = jnp.where(core == 1, 0.0, 1.0)
    w_all[:, :128] = (w_all[:, :128].astype(F32) * keep).astype(BF16)

    pass_on(4)
    multiply(6)

    cols = pl.ds(col, HALF)
    cuts = ((0, 512), (512, 512), (1024, 640))
    for low, size in cuts:
        go_out[:, low:low + size] = dot_nt(scaled[1, :, cols], w_all[low:low + size, :]).astype(BF16)
    go_copy = launch(go_out, go_in, GRAD, sibling)
    sent.append(go_copy)
    pass_on(5)
    multiply(7)
    finish_x(2)
    for low, size in cuts:
        go_own[:, low:low + size] = dot_nt(scaled[0, :, cols], w_all[low:low + size, :])
    pass_on(6)
    finish_x(3)
    finish_y(0)
    pass_on(7)
    go_copy.wait_recv()

    def grads(query, key, value, grad, probs):
        dprob = dot_nt(grad, value)
        delta = jnp.sum(probs * dprob, axis=1, keepdims=True)
        dscore = (probs * (dprob - delta) * FACTOR).astype(BF16)
        return dot_nn(dscore, key), dot_tn(dscore, query), dot_tn(probs.astype(BF16), grad)

    def backward(head, _):
        lanes = pl.ds(pl.multiple_of(head * HS, HS), HS)
        query, key, value = qkv[0, :, lanes], qkv[1, :, lanes], qkv[2, :, lanes]
        grad = (go_own[:, lanes] + go_in[:, lanes].astype(F32)).astype(BF16)
        main = grads(query[:MAIN], key[:MAIN], value[:MAIN], grad[:MAIN], p_main[head])
        tail = grads(query[MAIN:], key[MAIN:], value[MAIN:], grad[MAIN:], p_tail[head])
        for i in range(3):
            qkv[i, :MAIN, lanes] = main[i].astype(BF16)
            qkv[i, MAIN:, lanes] = tail[i].astype(BF16)
        return 0

    stores = []

    def back(low, high):
        lax.fori_loop(low, high, backward, 0)
        lanes = pl.ds(low * HS, (high - low) * HS)
        copy = pltpu.make_async_copy(qkv.at[:, :, lanes], grad_hbm.at[:, :, lanes], local.at[5 + len(stores)])
        copy.start()
        stores.append(copy)

    back(0, 4)
    finish_x(4)
    finish_x(5)
    back(4, 8)
    finish_x(6)
    finish_x(7)
    finish_y(1)
    back(8, HEADS)

    fin_copy = remote(total, total, FIN, sibling)
    for _, comes, copy in z_copies:
        pl.when(comes)(copy.wait_recv)

    def sum_z(term):
        for k in range(7):
            term = term + z_in[k].astype(F32)
        total[...] = term
        fin_copy.start()
        fin_copy.wait_send()

    @pl.when(mine & (z_hi == 0))
    def _():
        sum_z(za[z_lo % 2].astype(F32))

    @pl.when(mine & (z_hi == 1))
    def _():
        sum_z(jnp.concatenate([za[z_lo % 2, :, 384:], zb[z_lo % 2]], axis=1).astype(F32))

    @pl.when(jnp.logical_not(mine))
    def _():
        fin_copy.wait_recv()

    proj_ref[...] = total[...].T
    for copy in stores:
        copy.wait()
    for goes, _, copy in z_copies:
        pl.when(goes)(copy.wait_send)
    for copy in sent + att_copies + y_copies[0] + y_copies[1] + [c for hop in hops for c in hop]:
        copy.wait_send()


def local_part(query_key_value, cotangent, proj_weight, layer_scale, lengths):
    any_space = pl.BlockSpec(memory_space=pl.ANY)
    vmem = pl.BlockSpec(memory_space=pltpu.VMEM)
    grad, window = pl.pallas_call(
        kernel,
        out_shape=(
            jax.ShapeDtypeStruct((3, ROWS, HD), BF16),
            jax.ShapeDtypeStruct((512, SHARD), F32),
        ),
        in_specs=[any_space, any_space, any_space, any_space, pl.BlockSpec(memory_space=pltpu.SMEM)],
        out_specs=(any_space, vmem),
        scratch_shapes=[
            pltpu.VMEM((3, ROWS, HD), BF16),
            pltpu.VMEM((2, ROWS, D), BF16),
            pltpu.VMEM((1, D), F32),
            pltpu.VMEM((2, HD, ROWS), BF16),
            pltpu.VMEM((MAIN, MAIN), F32),
            pltpu.VMEM((TAIL, TAIL), F32),
            pltpu.VMEM((HEADS, MAIN, MAIN), F32),
            pltpu.VMEM((HEADS, TAIL, TAIL), F32),
            pltpu.VMEM((4, 4, SHARD, FIRST), BF16),
            pltpu.VMEM((4, 4, SHARD, LAST), BF16),
            pltpu.VMEM((HD, HALF), BF16),
            pltpu.VMEM((ROWS, HD), F32),
            pltpu.VMEM((ROWS, HD), BF16),
            pltpu.VMEM((ROWS, HD), BF16),
            pltpu.VMEM((4, 4, CHUNK, 512), BF16),
            pltpu.VMEM((4, 4, CHUNK, 384), BF16),
            pltpu.VMEM((4, 3, CHUNK, 512), BF16),
            pltpu.VMEM((4, 3, CHUNK, 384), BF16),
            pltpu.VMEM((4, CHUNK, 512), BF16),
            pltpu.VMEM((4, CHUNK, 384), BF16),
            pltpu.VMEM((3, CHUNK, 512), BF16),
            pltpu.VMEM((3, CHUNK, 384), BF16),
            pltpu.VMEM((2, SHARD, 512), BF16),
            pltpu.VMEM((2, SHARD, 384), BF16),
            pltpu.VMEM((7, SHARD, 512), BF16),
            pltpu.VMEM((SHARD, 512), F32),
            pltpu.SemaphoreType.DMA((N_MSG,)),
            pltpu.SemaphoreType.DMA((N_MSG,)),
            pltpu.SemaphoreType.DMA((8,)),
        ],
        compiler_params=pltpu.CompilerParams(
            collective_id=0, has_side_effects=True, vmem_limit_bytes=62 * 2**20
        ),
        name="attention_block",
    )(query_key_value, cotangent, proj_weight, layer_scale, lengths)
    dp = lax.axis_index("dp")
    start = (dp // 4) * 32 + ((dp // 2) % 2) * 16 + (dp % 2) * 200
    return grad, lax.dynamic_slice(window, (start, 0), (200, SHARD)).T


def solution(mesh):
    placed = (
        P(None, ("dp", "fsdp"), None),
        P(("dp", "fsdp"), None),
        P("fsdp", None),
        P(),
        P(None, "fsdp", None),
    )
    return jax.shard_map(
        local_part,
        mesh=mesh,
        in_specs=placed,
        out_specs=(P(None, ("dp", "fsdp"), None), P("fsdp", "dp")),
        check_vma=False,
    )
```

time: 118 us -> 95.3 us (0.81)
  Pallas kernels: 107 us -> 86.8 us
  local copies, waits for them, and re-layouts: 9.13 us -> 7.6 us
    pallas_call x1, Pallas kernels: 107 us -> 86.8 us  [local_part(): pl.pallas_call(kernel, out_shape=(jax.ShapeDtypeStruct((3, ROWS, HD), BF1...]
    reshape x2 -> x0, local copies, waits for them, and re-layouts: 2.68 us -> none  [the longest x1 1.35 us: local_part(): lengths.reshape(16, 4)]
    transpose x0 -> x1, local copies, waits for them, and re-layouts: none -> 1.55 us  [local_part(): return (grad, lax.dynamic_slice(window, (start, 0), (200, SHARD)).T)]
where the time goes in v2:
time: 95.3 us; the launch traced here: 95 us
  Pallas kernels  86.8 us (91%)
  local copies, waits for them, and re-layouts  7.6 us (8%)
    pallas_call x1, Pallas kernels, local_part(): pl.pallas_call(kernel, out_shape=(jax.ShapeDtypeStruct((3, ROWS, HD), BF1...  86.8 us
    unnamed x2, local copies, waits for them, and re-layouts  6.05 us

profile of v2, /device:TPU:1, one launch (start us, length us, event | category | flops | bytes accessed | tf_op | source)
XLA Modules:
  0.0 95.0 jit_solution(6317150830368202581)
XLA Ops:
  0.7 1.4 %copy.7.lens_ref = s32[16,1,4]{2,1,0:T(1,128)} copy(s32[16,1,4]{0,2,1:T(4,128)} %param.9) | data formatting | bytes 512 | tf_op args[4]
  2.0 86.8 %attention_block.1 = (bf16[3,448,1664]{2,1,0:T(8,128)(2,1)}, f32[512,104]{1,0:T(8,128)}) custom-call(bf16[3,448,1664]{2,1,0:T(8,128)(2,1)} %qkv_hbm.1, bf16[448,3200]{1,0:T(8,128)(2,1)} %cot_hbm.1, bf16[104,3200]{1,0:T(8,128)(2,1)} %w_hbm.1, f32[3200]{0:T(1024)} %scale_hbm.1, s32[16,1,4]{2,1,0:T(1,128)} %copy.7.lens_ref), custom_call_target="tpu_custom_call" | custom-call | tf_op jit(solution)/shard_map/attention_block/pallas_call | solution.py:416
  88.8 1.6 %dynamic-slice_bitcast_fusion = f32[104,200]{0,1:T(8,128)} fusion(f32[512,104]{1,0:T(8,128)} %get-tuple-element.5, s32[]{:T(128)S(6)} %select_n.25), kind=kLoop, calls=%fused_computation | loop fusion | bytes 166404 | tf_op jit(solution)/shard_map/transpose | solution.py:462
  90.4 4.7 %copy.9 = bf16[3,448,1664]{2,1,0:T(8,128)(2,1)} copy(bf16[3,448,1664]{2,1,0:T(8,128)(2,1)} %get-tuple-element.8) | data formatting | bytes 8945664

commit v3 on v2

--- a/solution.py
+++ b/solution.py
@@ -15,10 +15,10 @@
 ROWS = MAIN + TAIL
 SHARD = HD // 16
 HALF = 13 * 128
-FIRST = 7 * 128
+FIRST = 6 * 128
 LAST = HALF - FIRST
-WIN = 7 * 128
 STEP = 6 * 128
+SEAM = 5 * 128
 CHUNK = 208
 FACTOR = HS ** (-0.5)
 LOG2E = 1.4426950408889634
@@ -26,10 +26,12 @@
 F32 = jnp.float32
 BF16 = jnp.bfloat16
 
-A1, B1, A2, A3, B2, B3 = 0, 3, 7, 9, 11, 13
+A1, B1 = 0, 3
 COT, ATT, GRAD, XS, YS, ZS, FIN = 15, 20, 24, 25, 49, 55, 76
-N_MSG = 77
-PARTS = ((0, 512), (512, 384))
+SZ, SY, SX = 77, 89, 92
+A2, A3, B2, B3 = 99, 107, 111, 119
+N_MSG = 123
+PARTS = ((128, 384), (512, 256))
 
 
 def dot_nn(a, b):
@@ -47,7 +49,8 @@
 def kernel(
     qkv_hbm, cot_hbm, w_hbm, scale_hbm, lens_ref, grad_hbm, proj_ref,
     qkv, scaled, scale, att, bias_main, bias_tail, p_main, p_tail, w_a, w_b, w_all, go_own, go_out, go_in,
-    xa_own, xb_own, xa_in, xb_in, ya_own, yb_own, ya_in, yb_in, za, zb, z_in, total, send, recv, local,
+    xa_own, xb_own, xa_in, xb_in, ya_own, yb_own, ya_in, yb_in, za, zb, z_in, total,
+    turned, seam, sz_own, sz_in, sy_own, sy_in, sx_own, sx_in, send, recv, local,
 ):
     dp, member = lax.axis_index("dp"), lax.axis_index("fsdp")
     x, z_hi, core = dp // 4, (dp // 2) % 2, dp % 2
@@ -60,6 +63,9 @@
     def at_y(k):
         return (dp, lax.rem(y + k, 4) * 4 + z_lo)
 
+    def at_xz(k, flip):
+        return (lax.rem(x + k, 4) * 4 + (z_hi + flip) % 2 * 2 + core, member)
+
     def at_z(k):
         t = lax.rem(z + k, 8)
         return (x * 4 + (t // 4) * 2 + core, y * 4 + t % 4)
@@ -77,8 +83,16 @@
         copy.start()
         return copy
 
-    load_qkv = pltpu.make_async_copy(qkv_hbm, qkv, local.at[0])
-    load_qkv.start()
+    first = lax.rem(y + 1, 4)
+
+    def load_heads(low, count, index):
+        lanes = pl.ds(pl.multiple_of(low * HS, HS), count * HS)
+        copy = pltpu.make_async_copy(qkv_hbm.at[:, :, lanes], qkv.at[:, :, lanes], local.at[index])
+        copy.start()
+        return copy
+
+    loads = [load_heads(3 * first, 3, 8), load_heads(12, 1, 9)]
+    loads += [load_heads(3 * lax.rem(first + k, 4), 3, 9 + k) for k in (1, 2, 3)]
     load_scale = pltpu.make_async_copy(scale_hbm, scale.at[0], local.at[4])
     load_scale.start()
     load_cot = pltpu.make_async_copy(cot_hbm, scaled.at[0], local.at[1])
@@ -93,26 +107,10 @@
     load_b.start()
 
     peers = [sibling, at_x(1), at_x(3)] + [at_y(k) for k in (1, 2, 3)] + [at_z(k) for k in range(1, 8)]
+    peers += [at_x(2)] + [at_xz(k, 1) for k in (1, 2, 3)]
     barrier = pltpu.get_barrier_semaphore()
     for peer in peers:
         pl.semaphore_signal(barrier, inc=1, device_id=peer, device_id_type=MESH)
-    pl.semaphore_wait(barrier, len(peers))
-
-    windows = [pl.multiple_of(lax.rem(x + k, 4) * STEP, 128) for k in (2, 3, 1, 0)]
-    pieces = [pl.ds(low, STEP) for low in windows] + [pl.ds(D - 128, 128)]
-    cot_copies = [
-        launch(cot_hbm.at[:, piece], scaled.at[1, :, piece], COT + i, sibling) for i, piece in enumerate(pieces)
-    ]
-    sent = list(cot_copies)
-
-    gather_a = [launch(part_a, w_a.at[z_lo, y], A1 + i, at_y(k)) for i, k in enumerate((1, 3, 2))]
-    small = LAST // 2
-    gather_b = [launch(part_b, w_b.at[y, z_lo], B1 + i, at_z(k)) for i, k in enumerate((1, 7))]
-    for i, k in enumerate((2, 6)):
-        piece = w_hbm.at[:, pl.ds(col + FIRST + i * small, small)]
-        gather_b.append(launch(piece, w_b.at[y, z_lo, :, pl.ds(i * small, small)], B1 + 2 + i, at_z(k)))
-    sent += gather_a + gather_b
-
     first_count = lens_ref[dp, 0, 0]
     count_2, count_3 = lens_ref[dp, 0, 2], lens_ref[dp, 0, 3]
 
@@ -143,9 +141,7 @@
         norm = jnp.sum(weights, axis=1, keepdims=True)
         return weights * (1.0 / jnp.where(norm > 0.0, norm, 1.0))
 
-    load_qkv.wait()
-
-    def forward(head, _):
+    def forward(head):
         lanes = pl.ds(pl.multiple_of(head * HS, HS), HS)
         query, key, value = qkv[0, :, lanes], qkv[1, :, lanes], qkv[2, :, lanes]
         probs = soft(query[:MAIN], key[:MAIN], bias_main[...])
@@ -155,20 +151,58 @@
         out = dot_nn(probs.astype(BF16), value[:MAIN])
         out_t = dot_nn(probs_t.astype(BF16), value[MAIN:])
         att[0, lanes, :] = jnp.concatenate([out, out_t], axis=0).T.astype(BF16)
-        return 0
+
+    for copy in loads[:3]:
+        copy.wait()
+    forward(3 * first)
+    forward(3 * first + 1)
+    pl.semaphore_wait(barrier, len(peers))
+
+    windows = [pl.multiple_of(lax.rem(x + k, 4) * STEP, 128) for k in (2, 3, 1, 0)]
+    pieces = [pl.ds(low, STEP) for low in windows] + [pl.ds(D - 128, 128)]
+    cot_copies = []
+
+    def send_cot(low, high):
+        for i in range(low, high):
+            piece = pieces[i]
+            cot_copies.append(launch(cot_hbm.at[:, piece], scaled.at[1, :, piece], COT + i, sibling))
+
+    send_cot(0, 2)
+    sent = []
+
+    gather_a = [launch(part_a, w_a.at[z_lo, y], A1 + i, at_y(k)) for i, k in enumerate((1, 3, 2))]
+    gather_b = [launch(part_b, w_b.at[y, z_lo], B1 + i, at_z(k)) for i, k in enumerate((1, 7))]
+    for i, (k, low, size) in enumerate(((2, 0, 512), (6, 512, 384))):
+        piece = w_hbm.at[:, pl.ds(col + FIRST + low, size)]
+        gather_b.append(launch(piece, w_b.at[y, z_lo, :, pl.ds(low, size)], B1 + 2 + i, at_z(k)))
+    shards_a = [w_a.at[z_lo, lax.rem(y + k, 4)] for k in (0, 3, 1, 2)]
+    shards_b = [w_b.at[y, lax.rem(z_lo + k, 4)] for k in (0, 3, 1, 2)]
+    wide_a = [[launch(part_a, shards_a[0], A2 + 4 * i, at_z((1, 7)[i]))] for i in range(2)]
+    wide_b = [[launch(part_b, shards_b[0], B2 + 4 * i, at_y((1, 3)[i]))] for i in range(2)]
+    sent += gather_a + gather_b
 
     att_copies = []
 
     def heads(i):
         block = lax.rem(y + 1 + i, 4)
         low, high = 3 * block, 3 * block + 4
-        if i > 0:
+        if i == 0:
+            low = low + 2
+        else:
             low = low + jnp.where(block > 0, 1, 0)
         if i == 3:
             high = high - jnp.where(block < 3, 1, 0)
-        lax.fori_loop(low, high, forward, 0)
+
+        def pair(step, _):
+            forward(low + 2 * step)
+            forward(jnp.minimum(low + 2 * step + 1, high - 1))
+            return 0
+
+        lax.fori_loop(0, (high - low + 1) // 2, pair, 0)
         rows = pl.ds(pl.multiple_of(416 * block + CHUNK * (1 - core), 16), CHUNK)
         att_copies.append(launch(att.at[0, rows], att.at[1, rows], ATT + i, sibling))
+        if i == 0:
+            send_cot(2, 5)
 
     def scale_piece(part, piece):
         def one(step, _):
@@ -189,6 +223,9 @@
         part, at = i // 4, i % 4
         way = way_of(i)
         rows = pl.ds(pl.multiple_of(416 * lax.rem(y + 1 + at, 4) + CHUNK * core, 16), CHUNK)
+        if i == 0:
+            for j in range(4):
+                scale_piece(0, pieces[j])
         if part == 0:
             att_copies[at].wait_recv()
         hop = []
@@ -196,7 +233,6 @@
         order = (2, 4 - way, way, 0)
         for j, k in enumerate(order):
             if i == 0:
-                scale_piece(0, pieces[j])
                 cot_copies[j].wait_recv()
                 scale_piece(1, pieces[j])
             cols = pl.ds(pl.multiple_of(lax.rem(x + k, 4) * STEP + low, 128), size)
@@ -254,10 +290,10 @@
             if part == 0:
                 todo = [
                     (low, mine & (z_hi == 0), za.at[to_lo % 2], z_in.at[k - 1], ZS + k - 1),
-                    (high, mine & (z_hi == 1), za.at[to_lo % 2, :, pl.ds(384, 128)], z_in.at[k - 1, :, pl.ds(0, 128)], ZS + 6 + k),
+                    (high, mine & (z_hi == 1), za.at[to_lo % 2, :, pl.ds(256, 128)], z_in.at[k - 1, :, pl.ds(0, 128)], ZS + 6 + k),
                 ]
             else:
-                todo = [(high, mine & (z_hi == 1), zb.at[to_lo % 2], z_in.at[k - 1, :, pl.ds(128, 384)], ZS + 13 + k)]
+                todo = [(high, mine & (z_hi == 1), zb.at[to_lo % 2], z_in.at[k - 1, :, pl.ds(128, 256)], ZS + 13 + k)]
             for goes_now, comes, src, dst, index in todo:
                 copy = remote(src, dst, index, at_z(k))
                 pl.when(goes_now)(copy.start)
@@ -265,83 +301,115 @@
 
     mine = (z_lo // 2) == core
 
-    heads(0)
-    load_scale.wait()
-    load_cot.wait()
-    multiply(0)
-    heads(1)
-
-    load_a.wait()
-    load_b.wait()
-    for copy in gather_a:
-        copy.wait_recv()
-    wide_a = [launch(w_a.at[z_lo], w_a.at[z_lo], A2 + i, at_z(k)) for i, k in enumerate((1, 7))]
-    for copy in gather_b:
-        copy.wait_recv()
-    wide_b = [launch(w_b.at[y], w_b.at[y], B2 + i, at_y(k)) for i, k in enumerate((1, 3))]
-    sent += wide_a + wide_b
-
-    multiply(1)
-    pass_on(0)
-    heads(2)
-    multiply(2)
-    pass_on(1)
-    heads(3)
-    multiply(3)
-    pass_on(2)
-
-    wide_a[0].wait_recv()
-    behind, ahead = lax.rem(z_lo + 3, 4), lax.rem(z_lo + 1, 4)
-    far_a = [launch(w_a.at[behind, pl.ds(0, 2)], w_a.at[behind, pl.ds(0, 2)], A3, at_z(1))]
-    wide_a[1].wait_recv()
-    far_a.append(launch(w_a.at[ahead, pl.ds(2, 2)], w_a.at[ahead, pl.ds(2, 2)], A3 + 1, at_z(7)))
-    behind, ahead = lax.rem(y + 3, 4), lax.rem(y + 1, 4)
-    wide_b[0].wait_recv()
-    far_b = [launch(w_b.at[behind, pl.ds(0, 2)], w_b.at[behind, pl.ds(0, 2)], B3, at_y(1))]
-    wide_b[1].wait_recv()
-    far_b.append(launch(w_b.at[ahead, pl.ds(2, 2)], w_b.at[ahead, pl.ds(2, 2)], B3 + 1, at_y(3)))
-    sent += far_a + far_b
-
-    cot_copies[4].wait_recv()
-    scale_piece(0, pieces[4])
-    scale_piece(1, pieces[4])
-    multiply(4)
-    pass_on(3)
-    multiply(5)
-    finish_x(0)
-    finish_x(1)
-    for copy in far_a + far_b:
-        copy.wait_recv()
-
-    for block in range(4):
-        rows = slice(416 * block, 416 * block + 416)
-        left = jnp.concatenate([w_a[k, block].astype(F32) for k in range(4)], axis=0)
-        w_all[rows, :FIRST] = left.astype(BF16)
-        right = jnp.concatenate([w_b[block, k].astype(F32) for k in range(4)], axis=0)
-        w_all[rows, FIRST:] = right.astype(BF16)
-
-    keep = jnp.where(core == 1, 0.0, 1.0)
-    w_all[:, :128] = (w_all[:, :128].astype(F32) * keep).astype(BF16)
-
-    pass_on(4)
-    multiply(6)
-
-    cols = pl.ds(col, HALF)
-    cuts = ((0, 512), (512, 512), (1024, 640))
-    for low, size in cuts:
-        go_out[:, low:low + size] = dot_nt(scaled[1, :, cols], w_all[low:low + size, :]).astype(BF16)
-    go_copy = launch(go_out, go_in, GRAD, sibling)
-    sent.append(go_copy)
-    pass_on(5)
-    multiply(7)
-    finish_x(2)
-    for low, size in cuts:
-        go_own[:, low:low + size] = dot_nt(scaled[0, :, cols], w_all[low:low + size, :])
-    pass_on(6)
-    finish_x(3)
-    finish_y(0)
-    pass_on(7)
-    go_copy.wait_recv()
+    seam_sends, seam_comes, seam_y, seam_x = [], [[] for _ in range(4)], [], []
+
+    def gather_seam():
+        for part in range(2):
+            for k in range(5):
+                seam[part, :, k * 128:k * 128 + 128] = scaled[part, :, k * STEP:k * STEP + 128]
+
+    def seam_multiply(i):
+        rows = pl.ds(pl.multiple_of(416 * lax.rem(y + 1 + i, 4) + CHUNK * core, 16), CHUNK)
+        term = dot_nn(att[0, rows, :], seam[0]) + dot_nn(att[1, rows, :], seam[1])
+        for half in range(2):
+            sz_own[i, half] = term[half * SHARD:half * SHARD + SHARD].astype(BF16)
+        for d in (1, 2, 3):
+            to_lo = lax.rem(z_lo + d, 4)
+            goes = (to_lo // 2) == core
+            hop = (1, 2 if i < 2 else 6, 7)[d - 1]
+            copy = remote(sz_own.at[i, to_lo % 2], sz_in.at[i, d - 1], SZ + 3 * i + d - 1, at_z(hop))
+            pl.when(goes)(copy.start)
+            seam_sends.append((goes, copy))
+            seam_comes[i].append(copy)
+
+    def seam_to_y(i):
+        @pl.when(mine)
+        def _():
+            for copy in seam_comes[i]:
+                copy.wait_recv()
+            term = sz_own[i, z_lo % 2].astype(F32)
+            for k in range(3):
+                term = term + sz_in[i, k].astype(F32)
+            sy_own[i] = term.astype(BF16)
+
+        if i < 3:
+            copy = remote(sy_own.at[i], sy_in.at[i], SY + i, at_y(1 + i))
+            pl.when(mine)(copy.start)
+            seam_y.append(copy)
+
+    def seam_to_x():
+        @pl.when(mine)
+        def _():
+            term = sy_own[3].astype(F32)
+            for k in range(3):
+                seam_y[k].wait_recv()
+                term = term + sy_in[k].astype(F32)
+            sx_own[...] = term.astype(BF16)
+
+        for k in range(1, 8):
+            to_x, flip = lax.rem(x + k // 2, 4), k % 2
+            group = to_x + (z_hi + flip) % 2
+            src = sx_own.at[:, pl.ds(pl.multiple_of(group * 128, 128), 128)]
+            copy = remote(src, sx_in.at[k - 1], SX + k - 1, at_xz(k // 2, flip))
+            pl.when(mine)(copy.start)
+            seam_x.append(copy)
+
+    def widen(j):
+        if j == 1:
+            load_a.wait()
+            load_b.wait()
+        gather_a[j - 1].wait_recv()
+        gather_b[j - 1].wait_recv()
+        if j == 3:
+            gather_b[3].wait_recv()
+        for i in range(2):
+            wide_a[i].append(launch(shards_a[j], shards_a[j], A2 + 4 * i + j, at_z((1, 7)[i])))
+            wide_b[i].append(launch(shards_b[j], shards_b[j], B2 + 4 * i + j, at_y((1, 3)[i])))
+
+    far_copies = []
+
+    def far(j):
+        i = j // 2
+        wide_a[i][j].wait_recv()
+        wide_b[i][j].wait_recv()
+        shard = w_a.at[lax.rem(z_lo + (3, 1)[i], 4), lax.rem(y + (0, 3, 1, 2)[j], 4)]
+        far_copies.append(launch(shard, shard, A3 + j, at_z((1, 7)[i])))
+        shard = w_b.at[lax.rem(y + (3, 1)[i], 4), lax.rem(z_lo + (0, 3, 1, 2)[j], 4)]
+        far_copies.append(launch(shard, shard, B3 + j, at_y((1, 3)[i])))
+
+    def last_piece():
+        cot_copies[4].wait_recv()
+        scale_piece(0, pieces[4])
+        scale_piece(1, pieces[4])
+        gather_seam()
+
+    def collect():
+        for j in (0, 1):
+            wide_a[1][j].wait_recv()
+            wide_b[1][j].wait_recv()
+            wide_a[0][j + 2].wait_recv()
+            wide_b[0][j + 2].wait_recv()
+        for copy in far_copies:
+            copy.wait_recv()
+
+        for block in range(4):
+            rows = slice(416 * block, 416 * block + 416)
+            left = jnp.concatenate([w_a[k, block].astype(F32) for k in range(4)], axis=0)
+            w_all[rows, :FIRST] = left.astype(BF16)
+            right = jnp.concatenate([w_b[block, k].astype(F32) for k in range(4)], axis=0)
+            w_all[rows, FIRST:] = right.astype(BF16)
+
+        keep = jnp.where(core == 1, 0.0, 1.0)
+        w_all[:, :128] = (w_all[:, :128].astype(F32) * keep).astype(BF16)
+
+    def grad_out(part):
+        cols = pl.ds(col, HALF)
+        for low, size in ((0, 512), (512, 512), (1024, 640)):
+            term = dot_nt(scaled[part, :, cols], w_all[low:low + size, :])
+            if part == 1:
+                go_out[:, low:low + size] = term.astype(BF16)
+            else:
+                go_own[:, low:low + size] = term
 
     def grads(query, key, value, grad, probs):
         dprob = dot_nt(grad, value)
@@ -349,7 +417,7 @@
         dscore = (probs * (dprob - delta) * FACTOR).astype(BF16)
         return dot_nn(dscore, key), dot_tn(dscore, query), dot_tn(probs.astype(BF16), grad)
 
-    def backward(head, _):
+    def backward(head):
         lanes = pl.ds(pl.multiple_of(head * HS, HS), HS)
         query, key, value = qkv[0, :, lanes], qkv[1, :, lanes], qkv[2, :, lanes]
         grad = (go_own[:, lanes] + go_in[:, lanes].astype(F32)).astype(BF16)
@@ -358,55 +426,129 @@
         for i in range(3):
             qkv[i, :MAIN, lanes] = main[i].astype(BF16)
             qkv[i, MAIN:, lanes] = tail[i].astype(BF16)
-        return 0
 
     stores = []
 
     def back(low, high):
-        lax.fori_loop(low, high, backward, 0)
+        def pair(step, _):
+            backward(low + 2 * step)
+            backward(low + 2 * step + 1)
+            return 0
+
+        lax.fori_loop(0, (high - low) // 2, pair, 0)
+        if (high - low) % 2:
+            backward(high - 1)
         lanes = pl.ds(low * HS, (high - low) * HS)
-        copy = pltpu.make_async_copy(qkv.at[:, :, lanes], grad_hbm.at[:, :, lanes], local.at[5 + len(stores)])
+        copy = pltpu.make_async_copy(qkv.at[:, :, lanes], grad_hbm.at[:, :, lanes], local.at[13 + len(stores)])
         copy.start()
         stores.append(copy)
 
+    heads(0)
+    for copy in loads[3:]:
+        copy.wait()
+    load_scale.wait()
+    load_cot.wait()
+    heads(1)
+    multiply(0)
+    widen(1)
+    multiply(1)
+    heads(2)
+    pass_on(0)
+    heads(3)
+    multiply(2)
+    far(0)
+    widen(2)
+    last_piece()
+    multiply(3)
+    multiply(4)
+    widen(3)
+    far(1)
+    pass_on(2)
+    multiply(5)
+    pass_on(1)
+    far(2)
+    far(3)
+    pass_on(5)
+    seam_multiply(0)
+    seam_multiply(1)
+    pass_on(4)
+    pass_on(3)
+    seam_multiply(2)
+    multiply(6)
+    finish_x(1)
+    multiply(7)
+    finish_x(2)
+    seam_multiply(3)
+    finish_x(0)
+    finish_x(5)
+    collect()
+    grad_out(1)
+    go_copy = launch(go_out, go_in, GRAD, sibling)
+    finish_x(3)
+    seam_to_y(0)
+    pass_on(6)
+    finish_x(4)
+    grad_out(0)
+    go_copy.wait_recv()
+    seam_to_y(1)
+    pass_on(7)
+    seam_to_y(2)
+    finish_x(6)
+    finish_y(0)
     back(0, 4)
-    finish_x(4)
-    finish_x(5)
-    back(4, 8)
-    finish_x(6)
+    seam_to_y(3)
+    back(4, 6)
+    seam_to_x()
     finish_x(7)
     finish_y(1)
-    back(8, HEADS)
+    back(6, 12)
+    back(12, 13)
 
     fin_copy = remote(total, total, FIN, sibling)
     for _, comes, copy in z_copies:
         pl.when(comes)(copy.wait_recv)
-
-    def sum_z(term):
+    for copy in seam_x:
+        pl.when(mine)(copy.wait_recv)
+
+    def sum_seam():
+        term = sx_own[:, pl.ds(pl.multiple_of((x + z_hi) * 128, 128), 128)].astype(F32)
+        for k in range(7):
+            term = term + sx_in[k].astype(F32)
+        return term
+
+    def sum_z(term, low, high):
         for k in range(7):
             term = term + z_in[k].astype(F32)
-        total[...] = term
+        total[:, low:high] = term
         fin_copy.start()
         fin_copy.wait_send()
 
     @pl.when(mine & (z_hi == 0))
     def _():
-        sum_z(za[z_lo % 2].astype(F32))
+        total[:, :128] = sum_seam()
+        sum_z(za[z_lo % 2].astype(F32), 128, 512)
 
     @pl.when(mine & (z_hi == 1))
     def _():
-        sum_z(jnp.concatenate([za[z_lo % 2, :, 384:], zb[z_lo % 2]], axis=1).astype(F32))
+        total[:, 384:] = sum_seam()
+        sum_z(jnp.concatenate([za[z_lo % 2, :, 256:], zb[z_lo % 2]], axis=1).astype(F32), 0, 384)
 
     @pl.when(jnp.logical_not(mine))
     def _():
         fin_copy.wait_recv()
 
-    proj_ref[...] = total[...].T
+    turned[...] = total[...].T
+    start = x * 32 + z_hi * 16 + core * 200
+    proj_ref[...] = turned[pl.ds(pl.multiple_of(start, 8), 200), :]
     for copy in stores:
         copy.wait()
     for goes, _, copy in z_copies:
         pl.when(goes)(copy.wait_send)
-    for copy in sent + att_copies + y_copies[0] + y_copies[1] + [c for hop in hops for c in hop]:
+    for goes, copy in seam_sends:
+        pl.when(goes)(copy.wait_send)
+    for copy in seam_y + seam_x:
+        pl.when(mine)(copy.wait_send)
+    for copy in sent + [go_copy] + far_copies + cot_copies + wide_a[0] + wide_a[1] + wide_b[0] + wide_b[1] + att_copies + y_copies[0] + y_copies[1] + [c for hop in hops for c in hop]:
         copy.wait_send()
 
 
@@ -417,7 +559,7 @@
         kernel,
         out_shape=(
             jax.ShapeDtypeStruct((3, ROWS, HD), BF16),
-            jax.ShapeDtypeStruct((512, SHARD), F32),
+            jax.ShapeDtypeStruct((200, SHARD), F32),
         ),
         in_specs=[any_space, any_space, any_space, any_space, pl.BlockSpec(memory_space=pltpu.SMEM)],
         out_specs=(any_space, vmem),
@@ -436,30 +578,36 @@
             pltpu.VMEM((ROWS, HD), F32),
             pltpu.VMEM((ROWS, HD), BF16),
             pltpu.VMEM((ROWS, HD), BF16),
-            pltpu.VMEM((4, 4, CHUNK, 512), BF16),
             pltpu.VMEM((4, 4, CHUNK, 384), BF16),
-            pltpu.VMEM((4, 3, CHUNK, 512), BF16),
+            pltpu.VMEM((4, 4, CHUNK, 256), BF16),
             pltpu.VMEM((4, 3, CHUNK, 384), BF16),
-            pltpu.VMEM((4, CHUNK, 512), BF16),
+            pltpu.VMEM((4, 3, CHUNK, 256), BF16),
             pltpu.VMEM((4, CHUNK, 384), BF16),
-            pltpu.VMEM((3, CHUNK, 512), BF16),
+            pltpu.VMEM((4, CHUNK, 256), BF16),
             pltpu.VMEM((3, CHUNK, 384), BF16),
-            pltpu.VMEM((2, SHARD, 512), BF16),
+            pltpu.VMEM((3, CHUNK, 256), BF16),
             pltpu.VMEM((2, SHARD, 384), BF16),
-            pltpu.VMEM((7, SHARD, 512), BF16),
+            pltpu.VMEM((2, SHARD, 256), BF16),
+            pltpu.VMEM((7, SHARD, 384), BF16),
             pltpu.VMEM((SHARD, 512), F32),
+            pltpu.VMEM((512, SHARD), F32),
+            pltpu.VMEM((2, ROWS, SEAM), BF16),
+            pltpu.VMEM((4, 2, SHARD, SEAM), BF16),
+            pltpu.VMEM((4, 3, SHARD, SEAM), BF16),
+            pltpu.VMEM((4, SHARD, SEAM), BF16),
+            pltpu.VMEM((3, SHARD, SEAM), BF16),
+            pltpu.VMEM((SHARD, SEAM), BF16),
+            pltpu.VMEM((7, SHARD, 128), BF16),
             pltpu.SemaphoreType.DMA((N_MSG,)),
             pltpu.SemaphoreType.DMA((N_MSG,)),
-            pltpu.SemaphoreType.DMA((8,)),
+            pltpu.SemaphoreType.DMA((18,)),
         ],
         compiler_params=pltpu.CompilerParams(
             collective_id=0, has_side_effects=True, vmem_limit_bytes=62 * 2**20
         ),
         name="attention_block",
     )(query_key_value, cotangent, proj_weight, layer_scale, lengths)
-    dp = lax.axis_index("dp")
-    start = (dp // 4) * 32 + ((dp // 2) % 2) * 16 + (dp % 2) * 200
-    return grad, lax.dynamic_slice(window, (start, 0), (200, SHARD)).T
+    return grad, window.T
 
 
 def solution(mesh):

time: 95.3 us -> 84 us (0.88)
  Pallas kernels: 86.8 us -> 76.5 us
    pallas_call x1, Pallas kernels: 86.8 us -> 76.5 us  [local_part(): pl.pallas_call(kernel, out_shape=(jax.ShapeDtypeStruct((3, ROWS, HD), BF1...]
    transpose x1 -> x0, local copies, waits for them, and re-layouts: 1.55 us -> none  [local_part(): return (grad, lax.dynamic_slice(window, (start, 0), (200, SHARD)).T)]
    unnamed x2 -> x5, local copies, waits for them, and re-layouts: 6.05 us -> 6.73 us
where the time goes in v3:
time: 84 us; the launch traced here: 83.9 us
  Pallas kernels  76.5 us (91%)
  local copies, waits for them, and re-layouts  6.73 us (8%)
    pallas_call x1, Pallas kernels, local_part(): pl.pallas_call(kernel, out_shape=(jax.ShapeDtypeStruct((3, ROWS, HD), BF1...  76.5 us
    unnamed x5, local copies, waits for them, and re-layouts  6.73 us

profile of v3, /device:TPU:1, one launch (start us, length us, event | category | flops | bytes accessed | tf_op | source)
XLA Modules:
  0.0 83.9 jit_solution(6680919487322266536)
XLA Ops:
  0.6 1.4 %copy.7.lens_ref = s32[16,1,4]{2,1,0:T(1,128)} copy(s32[16,1,4]{0,2,1:T(4,128)} %param.9) | data formatting | bytes 512 | tf_op args[4]
  2.0 76.5 %attention_block.1 = (bf16[3,448,1664]{2,1,0:T(8,128)(2,1)}, f32[200,104]{1,0:T(8,128)}) custom-call(bf16[3,448,1664]{2,1,0:T(8,128)(2,1)} %qkv_hbm.1, bf16[448,3200]{1,0:T(8,128)(2,1)} %cot_hbm.1, bf16[104,3200]{1,0:T(8,128)(2,1)} %w_hbm.1, f32[3200]{0:T(1024)} %scale_hbm.1, s32[16,1,4]{2,1,0:T(1,128)} %copy.7.lens_ref), custom_call_target="tpu_custom_call" | custom-call | tf_op jit(solution)/shard_map/attention_block/pallas_call | solution.py:558
  78.5 0.0 copy-start
  78.5 4.7 %copy.10 = bf16[3,448,1664]{2,1,0:T(8,128)(2,1)} copy(bf16[3,448,1664]{2,1,0:T(8,128)(2,1)} %get-tuple-element.8) | data formatting | bytes 8945664
  83.2 0.0 copy-done
  83.2 0.6 copy.11
Async XLA Ops:
  78.5 4.7 %copy-start = (f32[200,104]{1,0:T(8,128)S(1)}, f32[200,104]{1,0:T(8,128)}, u32[]{:S(2)}) copy-start(f32[200,104]{1,0:T(8,128)} %get-tuple-element.5) | copy-start | bytes 249604
